TPU v7x, 32 devices: a whole 2x2x4 slice. The times are simulated.
32 devices in a mesh: dp: 16 (over z, x, core), mp: 2 (over y).
Axes of the slice: x: 2, y: 2, z: 4, core: 2. Of those that a mesh axis runs over, the one named last changes fastest.
Arguments:
- block_in: bfloat16 [16384, 768], P(('dp', 'mp')), may hold values from -6 to 6
- cotangent: bfloat16 [16384, 768], P(('dp', 'mp')), may hold values from -6 to 6
- lengths: int32 [16, 21], P('dp'), may hold values from 0 to 256, as said below
- token_mask: int32 [16, 1024], P('dp'), may hold values 0 or 1
- ln1_gain: float32 [768], replicated, may hold values from 0.25 to 1.75
- ln1_bias: float32 [768], replicated, may hold values from -3 to 3
- w_qkv: bfloat16 [768, 3, 768], P(None, None, 'mp'), may hold values from -0.3125 to 0.3125
- b_qv: float32 [2, 768], P(None, 'mp'), may hold values from -3 to 3
- w_out: bfloat16 [768, 768], P('mp'), may hold values from -1.5 to 1.5
- b_out: float32 [768], replicated, may hold values from -3 to 3
- ln2_gain: float32 [768], replicated, may hold values from 0.25 to 1.75
- ln2_bias: float32 [768], replicated, may hold values from -3 to 3
- w_up: bfloat16 [768, 3072], P(None, 'mp'), may hold values from -0.21875 to 0.21875
- b_up: float32 [3072], P('mp'), may hold values from -3 to 3
- w_down: bfloat16 [3072, 768], P('mp'), may hold values from -0.109375 to 0.109375
- b_down: float32 [768], replicated, may hold values from -3 to 3
Outputs:
- block_out: bfloat16 [16384, 768], P(('dp', 'mp'))
- d_block_in: bfloat16 [16384, 768], P(('dp', 'mp'))
- d_ln1_gain: float32 [768], replicated
- d_ln1_bias: float32 [768], replicated
- d_w_qkv: float32 [768, 3, 768], P(None, None, 'mp')
- d_b_qv: float32 [2, 768], P(None, 'mp')
- d_w_out: float32 [768, 768], P('mp')
- d_b_out: float32 [768], replicated
- d_ln2_gain: float32 [768], replicated
- d_ln2_bias: float32 [768], replicated
- d_w_up: float32 [768, 3072], P(None, 'mp')
- d_b_up: float32 [3072], P('mp')
- d_w_down: float32 [3072, 768], P('mp')
- d_b_down: float32 [768], replicated
Inputs may be any that keep to these rules, and one draw needn't show every extreme that they name: `lengths`: row r lists, in order, the patch counts of the images packed into packed row r of 1024 tokens: every nonzero entry is 49, 196 or 256, zero entries come only after the nonzero ones, the entries of a row sum to at most 1024, and the last entry of every row is 0.
All inputs are finite; a program needn't handle non-finite values. No bound on the sum of `token_mask` on one device may be relied on, other than what follows from the above.
Results may differ from a plain program's by a relative error of at most 0.017.
The roundings to bfloat16 on the way count: a program that leaves them out, or rounds other values in their place, can miss the bound.
Values may be sent and summed in bfloat16 or wider, within the bound.
A program may use at most 192 MiB of HBM per device.

v0:
```python
import functools
import jax
import jax.numpy as jnp
from jax import lax
from jax.experimental import pallas as pl
from jax.experimental.pallas import tpu as pltpu
from jax.sharding import PartitionSpec as P

HEAD_DIM = 64
MESH = pl.DeviceIdType.MESH
WIDE = 768
GROUPS = 3
LANES = 128


def ring_place(chip, chips):
    return jnp.where(chip % 2 == 0, chip // 2, chips - 1 - chip // 2)


def ring_chip(place, chips):
    return jnp.where(place < chips // 2, 2 * place, 2 * (chips - 1 - place) + 1)


def send_slots(chips):
    return min(chips, 8)


def whole_blocks(rows, n_dp):
    unit = 16 * n_dp
    return -(-rows // unit) * unit


class Here:
    def __init__(self, chips):
        dp, mp = lax.axis_index("dp"), lax.axis_index("mp")
        self.chips = chips
        self.core, chip = dp % 2, dp // 2
        self.place = ring_place(chip, chips)
        self.following = {"dp": ring_chip((self.place + 1) % chips, chips) * 2 + self.core}
        self.previous = {"dp": ring_chip((self.place + chips - 1) % chips, chips) * 2 + self.core}
        self.sibling = {"dp": chip * 2 + 1 - self.core}
        self.partner = {"mp": 1 - mp}
        self.side = chip % 2
        self.beside = {"dp": (chip + 1 - 2 * self.side) * 2 + self.core}


def remote(src, dst, send, recv, to):
    return pltpu.make_async_remote_copy(
        src_ref=src, dst_ref=dst, send_sem=send, recv_sem=recv, device_id=to, device_id_type=MESH
    )


class Segment:
    def __init__(self, here, base, rows, grads, from_core, landed, result, sems, own_sems=None):
        self.here, self.base, self.chips = here, base, here.chips
        self.block = rows // (2 * here.chips)
        self.slots = send_slots(here.chips)
        self.own_sems = own_sems
        self.grads, self.from_core, self.landed, self.result = grads, from_core, landed, result
        (
            self.core_send,
            self.core_recv,
            self.rs_send,
            self.rs_recv,
            self.ag_send,
            self.ag_recv,
            self.pair_send,
            self.pair_recv,
        ) = sems

    def rows_of(self, core, blk):
        start = self.base + (core * self.chips + blk) * self.block
        return pl.ds(pl.multiple_of(start, 16), self.block)

    def near_rows(self, blk):
        start = self.base // 2 + blk * self.block
        return pl.ds(pl.multiple_of(start, 16), self.block)

    def columns(self, ring):
        return pl.ds(ring * LANES, LANES)

    def rs_block(self, ring, step):
        if ring < GROUPS:
            return (self.here.place + 2 * self.chips - 1 - step) % self.chips
        return (self.here.place + 1 + step) % self.chips

    def ag_block(self, ring, step):
        if ring < GROUPS:
            return (self.here.place + self.chips - step) % self.chips
        return (self.here.place + step) % self.chips

    def toward(self, ring):
        return self.here.following if ring < GROUPS else self.here.previous

    def core_copy(self, half, step):
        blk = self.rs_block(half * GROUPS, step)
        cols = pl.ds(half * GROUPS * LANES, GROUPS * LANES)
        return remote(
            self.grads.at[self.rows_of(1 - self.here.core, blk), cols],
            self.from_core.at[self.near_rows(blk), cols],
            self.core_send.at[half, step],
            self.core_recv.at[half, step],
            self.here.sibling,
        )

    def rs_copy(self, ring, step):
        cols = self.columns(ring)
        return remote(
            self.grads.at[self.rows_of(self.here.core, self.rs_block(ring, step)), cols],
            self.landed.at[step, :, cols],
            self.rs_send.at[ring, step % self.slots],
            self.rs_recv.at[ring, step],
            self.toward(ring),
        )

    def result_copy(self, ring, step, send, recv, to, wide=1):
        rows = self.rows_of(self.here.core, self.ag_block(ring, step))
        cols = pl.ds(ring * LANES, wide * LANES)
        spot = self.result.at[rows, cols]
        own = self.own_sems is not None and isinstance(step, int) and step == 0
        held = self.grads.at[rows, cols] if own else spot
        lane = ring // wide
        return remote(held, spot, send.at[lane, step % self.slots], recv.at[lane, step], to)

    def own_copy(self, ring):
        spot = (self.rows_of(self.here.core, self.here.place), self.columns(ring))
        return pltpu.make_async_copy(
            self.grads.at[spot], self.result.at[spot], self.own_sems.at[ring]
        )

    def ag_copy(self, ring, step):
        return self.result_copy(ring, step, self.ag_send, self.ag_recv, self.toward(ring))

    def pair_copy(self, way, step):
        to = self.here.sibling
        return self.result_copy(way * GROUPS, step, self.pair_send, self.pair_recv, to, GROUPS)

    def pass_on(self, group, step):
        if group == GROUPS - 1:
            self.send(self.pair_copy, 0, step)
            self.send(self.pair_copy, 1, step)

    def summed(self, ring, step, first):
        blk = self.rs_block(ring, step)
        rows, cols = self.rows_of(self.here.core, blk), self.columns(ring)
        value = self.grads[rows, cols].astype(jnp.float32)
        value = value + self.from_core[self.near_rows(blk), cols].astype(jnp.float32)
        if not first:
            value = value + self.landed[step - 1, :, cols].astype(jnp.float32)
        return rows, cols, value.astype(jnp.bfloat16)

    def send(self, copy, ring, step):
        if self.slots < self.chips:

            @pl.when(step >= self.slots)
            def _():
                copy(ring, step - self.slots).wait_send()

        copy(ring, step).start()

    def swap_cores(self):
        def start(step, carry):
            self.core_copy(0, step).start()
            self.core_copy(1, step).start()
            return carry

        lax.fori_loop(0, self.chips, start, 0)

    def wait_core(self, step):
        self.core_copy(0, step).wait_recv()
        self.core_copy(1, step).wait_recv()

    def begin(self):
        self.wait_core(0)
        for group in range(GROUPS):
            for ring in (group, group + GROUPS):
                rows, cols, value = self.summed(ring, 0, True)
                self.grads[rows, cols] = value
                self.send(self.rs_copy, ring, 0)

    def stage(self, group, step):
        n = self.chips
        rings = (group, group + GROUPS)

        @pl.when(step <= n - 2)
        def _():
            if group == 0:
                self.wait_core(step)
            for ring in rings:
                self.rs_copy(ring, step - 1).wait_recv()
                rows, cols, value = self.summed(ring, step, False)
                self.grads[rows, cols] = value
                self.send(self.rs_copy, ring, step)

        @pl.when(step == n - 1)
        def _():
            if group == 0:
                self.wait_core(n - 1)
            for ring in rings:
                self.rs_copy(ring, n - 2).wait_recv()
                rows, cols, value = self.summed(ring, n - 1, False)
                if self.own_sems is None:
                    self.result[rows, cols] = value
                else:
                    self.grads[rows, cols] = value
                    self.own_copy(ring).start()
                self.send(self.ag_copy, ring, 0)
            self.pass_on(group, 0)

        @pl.when((step >= n) & (step <= 2 * n - 3))
        def _():
            for ring in rings:
                self.ag_copy(ring, step - n).wait_recv()
                self.send(self.ag_copy, ring, step - n + 1)
            self.pass_on(group, step - n + 1)

        @pl.when(step == 2 * n - 2)
        def _():
            for ring in rings:
                self.ag_copy(ring, n - 2).wait_recv()
            self.pass_on(group, n - 1)

    def stages(self, first, last):
        def run(step, carry):
            for group in range(GROUPS):
                self.stage(group, step)
            return carry

        lax.fori_loop(first, last, run, 0)

    def arrive(self):
        def run(step, carry):
            for way in range(2):
                self.pair_copy(way, step).wait_recv()
            return carry

        lax.fori_loop(0, self.chips, run, 0)
        if self.own_sems is not None:
            for ring in range(2 * GROUPS):
                self.own_copy(ring).wait()

    def drain(self):
        def cores(step, carry):
            self.core_copy(0, step).wait_send()
            self.core_copy(1, step).wait_send()
            return carry

        def pairs(step, carry):
            for way in range(2):
                self.pair_copy(way, step).wait_send()
            return carry

        def ring_steps(step, carry):
            for ring in range(2 * GROUPS):
                self.rs_copy(ring, step).wait_send()
                self.ag_copy(ring, step).wait_send()
            return carry

        n, slots = self.chips, self.slots
        lax.fori_loop(0, n, cores, 0)
        lax.fori_loop(n - slots, n, pairs, 0)
        lax.fori_loop(max(n - 1 - slots, 0), n - 1, ring_steps, 0)


def segment_sems(chips):
    dma = pltpu.SemaphoreType.DMA
    rings = 2 * GROUPS
    slots = send_slots(chips)
    both = [dma((rings, slots)), dma((rings, chips))]
    return [dma((2, chips))] * 2 + both * 2 + [dma((2, slots)), dma((2, chips))]


class Small:
    def __init__(self, here, from_core, from_mp, every, pair_sems, ring_sems):
        self.here, self.from_core, self.from_mp, self.every = here, from_core, from_mp, every
        self.pair_sems, self.ring_sems = pair_sems, ring_sems
        self.forward = here.chips // 2
        self.backward = here.chips - 1 - self.forward

    def pair(self, which, src, dst, to):
        return remote(src, dst, self.pair_sems.at[0, which], self.pair_sems.at[1, which], to)

    def start(self, src):
        self.src = src
        self.to_core = self.pair(0, src, self.from_core, self.here.sibling)
        self.to_core.start()

    def core_done(self):
        self.to_core.wait()
        place = self.here.place
        self.every[place] = self.src[...] + self.from_core[...]
        spot = self.every.at[place, pl.ds(8, 8)]
        self.to_mp = self.pair(1, spot, self.from_mp, self.here.partner)
        self.to_mp.start()

    def mp_done(self):
        self.to_mp.wait()
        place = self.here.place
        self.every[place, pl.ds(8, 8)] = self.every[place, pl.ds(8, 8)] + self.from_mp[...]
        self.step(0, 0).start()
        if self.backward:
            self.step(1, 0).start()

    def step(self, way, step):
        n = self.here.chips
        at = (self.here.place + n - step) % n if way == 0 else (self.here.place + step) % n
        spot = self.every.at[at]
        to = self.here.following if way == 0 else self.here.previous
        sems = self.ring_sems
        return remote(spot, spot, sems.at[0, way, step], sems.at[1, way, step], to)

    def hop(self, step):
        for way, count in ((0, self.forward), (1, self.backward)):

            @pl.when(step < count)
            def _():
                self.step(way, step - 1).wait_recv()
                self.step(way, step).start()

    def finish(self, out, hops):
        def run(step, carry):
            self.hop(step)
            return carry

        if hops < self.forward:
            lax.fori_loop(hops, self.forward, run, 0)
        self.step(0, self.forward - 1).wait_recv()
        if self.backward:
            self.step(1, self.backward - 1).wait_recv()
        out[...] = self.every[0]

        def add(chip, carry):
            out[...] += self.every[chip]
            return carry

        lax.fori_loop(1, self.here.chips, add, 0)

        def sent(way, count):
            def run(step, carry):
                self.step(way, step).wait_send()
                return carry

            lax.fori_loop(0, count, run, 0)

        sent(0, self.forward)
        sent(1, self.backward)


def small_scratch(chips):
    dma = pltpu.SemaphoreType.DMA
    return [
        pltpu.VMEM((16, WIDE), jnp.float32),
        pltpu.VMEM((8, WIDE), jnp.float32),
        pltpu.VMEM((chips, 16, WIDE), jnp.float32),
        dma((2, 2)),
        dma((2, 2, chips)),
    ]


LOW = jnp.bfloat16
F32 = jnp.float32
HALF = 512
TILE = 256
SPAN = 128
STRIP = 32
HIDDEN = 256
EPS = 1e-06
FAR = -1e30
SCALE = HEAD_DIM**-0.5
NT = (((1,), (1,)), ((), ()))
TN = (((0,), (0,)), ((), ()))


def nt_dot(a, b):
    return lax.dot_general(a, b, NT, preferred_element_type=F32)


def tn_dot(a, b):
    return lax.dot_general(a, b, TN, preferred_element_type=F32)


def dot(a, b):
    return jnp.dot(a, b, preferred_element_type=F32)


def normal_parts(values):
    centred = values - jnp.mean(values, axis=-1, keepdims=True)
    spread = jnp.mean(centred * centred, axis=-1, keepdims=True)
    return centred, lax.rsqrt(spread + EPS)


def norm_back(d_out, unit, inverse, gain):
    e = d_out * gain
    share = e - jnp.mean(e, -1, keepdims=True)
    return inverse * (share - unit * jnp.mean(e * unit, -1, keepdims=True))


def column_sum(values):
    return jnp.sum(values, axis=0, keepdims=True)


def split_heads(pair):
    low_lanes = lax.broadcasted_iota(jnp.int32, pair.shape, 1) < HEAD_DIM
    zero = jnp.zeros_like(pair)
    return jnp.concatenate([jnp.where(low_lanes, pair, zero), jnp.where(low_lanes, zero, pair)])


def own_blocks(both):
    return jnp.concatenate([both[:HEAD_DIM, :SPAN], both[HEAD_DIM:, SPAN:]], axis=0)


def twice(values):
    return jnp.concatenate([values, values], axis=1)


SCRATCH = (
    "x_own", "h1", "cot", "h2", "wq", "w_mine", "w_got", "q", "k", "v", "att32", "att_send",
    "att_got", "lse", "key_code", "query_seg", "bias", "middle", "out_sum", "out_send", "out_got",
    "dh_own", "dh2_send", "dh2_got", "d_branch", "d_att", "go_send", "go_core", "go_got",
    "small_ref", "grads", "from_core", "result", "landed_m", "landed_q", "local_sems", "swap_sems",
    "pass_sems", "own_sems",
)


def twice_rows(values):
    return jnp.concatenate([values[0:1], values[1:2]], axis=1)


def fold(values, op, rows=8):
    while values.shape[0] > rows:
        half = values.shape[0] // 2
        values = op(values[:half], values[half:])
    return values


def strips(rows):
    return [slice(at, at + STRIP) for at in range(0, rows, STRIP)]


def result_in_hbm(chips):
    return chips > 8


class Names:
    pass


def block_kernel(chips, sizes, *refs):
    (
        x_hbm,
        cot_hbm,
        wq_hbm,
        w_out_hbm,
        up_hbm,
        down_hbm,
        lengths,
        mask_ref,
        gain1,
        bias1,
        b_qv,
        b_out,
        gain2,
        bias2,
        b_up,
        b_down,
        summed_ref,
        out_ref,
        dx_ref,
        small_out,
    ) = refs[:20]
    m = Names()
    for name, ref in zip(SCRATCH, refs[20:]):
        setattr(m, name, ref)
    more = refs[20 + len(SCRATCH) :]
    sems_m, sems_q, small_refs = more[:8], more[8:16], more[16:]
    rows_m, rows_q = sizes
    here = Here(chips)
    direct = result_in_hbm(chips)
    result = summed_ref if direct else m.result
    ring_m = Segment(
        here, 0, rows_m, m.grads, m.from_core, m.landed_m, result, sems_m,
        m.own_sems.at[0] if direct else None,
    )
    ring_q = Segment(
        here, rows_m, rows_q, m.grads, m.from_core, m.landed_q, result, sems_q,
        m.own_sems.at[1] if direct else None,
    )
    small = Small(here, *small_refs)
    width = m.k.shape[1]
    pairs = width // 128
    row_len = 2 * HALF
    hidden = up_hbm.shape[1]
    blocks = row_len // SPAN

    def local(which, src, dst):
        return pltpu.make_async_copy(src, dst, m.local_sems.at[which])

    def swapped(which, src, dst):
        return remote(src, dst, m.swap_sems.at[0, which], m.swap_sems.at[1, which], here.partner)

    def part(chunk):
        return pl.ds(pl.multiple_of(chunk * TILE, TILE), TILE)

    def other(chunk):
        return pl.ds(pl.multiple_of(HALF + chunk * TILE, TILE), TILE)

    def x_swap(chunk):
        return swapped(chunk, x_hbm.at[part(chunk)], m.h1.at[other(chunk)])

    def cot_swap(chunk):
        return swapped(2 + chunk, cot_hbm.at[part(chunk)], m.cot.at[other(chunk)])

    def h2_swap(chunk):
        return swapped(4 + chunk, m.h2.at[part(chunk)], m.h2.at[other(chunk)])

    def dh2_swap(chunk):
        return swapped(6 + chunk, m.dh2_send.at[part(chunk)], m.dh2_got.at[part(chunk)])

    def out_swap(chunk):
        return swapped(8 + chunk, m.out_send.at[part(chunk)], m.out_got.at[part(chunk)])

    def dh1_swap(chunk):
        return swapped(10 + chunk, m.dh2_send.at[part(chunk)], m.dh2_got.at[part(chunk)])

    quarter = width // 2
    w_rows = pl.ds(pl.multiple_of(here.core * quarter, 16), quarter)
    piece = pl.ds(pl.multiple_of((here.core * 2 + here.side) * (quarter // 2), 16), quarter // 2)
    w_swap = swapped(12, w_out_hbm.at[piece], m.w_got.at[piece])
    w_share = remote(
        m.w_got.at[piece], m.w_got.at[piece], m.pass_sems.at[4], m.pass_sems.at[5], here.beside
    )
    w_pass = remote(
        m.w_got.at[w_rows], m.w_got.at[w_rows], m.pass_sems.at[0], m.pass_sems.at[1], here.sibling
    )
    att_swap = swapped(13, m.att_send, m.att_got)
    da_swap = swapped(14, m.att_send, m.d_att.at[pl.ds(HALF, HALF)])
    other_rows = pl.ds(pl.multiple_of((1 - here.core) * quarter, 16), quarter)
    go_pass = remote(
        m.go_send.at[other_rows], m.go_core, m.pass_sems.at[2], m.pass_sems.at[3], here.sibling
    )
    go_swap = swapped(15, m.go_core, m.go_got)

    def as_row(ref):
        return ref[...].reshape(1, ref.shape[0])

    load_x = local(0, x_hbm, m.x_own)
    load_wq = local(1, wq_hbm, m.wq)
    load_w = local(2, w_out_hbm, m.w_mine)
    load_cot = local(3, cot_hbm, m.cot.at[pl.ds(0, HALF)])
    for load in (load_x, load_wq, load_w, load_cot):
        load.start()
    barrier = pltpu.get_barrier_semaphore()
    near = (here.sibling, here.following, here.previous, here.partner, here.beside)
    for device in near:
        pl.semaphore_signal(barrier, inc=1, device_id=device, device_id_type=MESH)
    pl.semaphore_wait(barrier, len(near))
    x_swap(0).start()

    shift = lax.axis_index("mp") * HALF
    ends, total = [], lengths[0, 0]
    for slot in range(lengths.shape[1]):
        ends.append(total)
        if slot + 1 < lengths.shape[1]:
            total = total + lengths[0, slot + 1]

    def segment(shape, axis):
        at = (lax.broadcasted_iota(jnp.int32, shape, axis) + shift) % row_len
        found = jnp.zeros(shape, jnp.int32)
        for end in ends:
            found = found + (at >= end).astype(jnp.int32)
        return found

    seg_row = segment((1, row_len), 1)
    for block in range(blocks):
        m.query_seg[block] = seg_row[:, block * SPAN : (block + 1) * SPAN]
    mask = mask_ref[...]
    turned = jnp.concatenate([mask[:, HALF:], mask[:, :HALF]], axis=1)
    mask = jnp.where(shift == 0, mask, turned)
    code = jnp.where(mask == 1, seg_row, -1).astype(F32)
    m.key_code[...] = jnp.broadcast_to(code, (8, row_len)).T[:, :1].astype(jnp.int32)

    def project(values, rows):
        centred, inverse = normal_parts(values.astype(F32))
        h1 = (centred * inverse * as_row(gain1) + as_row(bias1)).astype(LOW)
        m.h1[rows] = h1
        m.q[rows] = ((dot(h1, m.wq[0]) + b_qv[0:1]) * SCALE).astype(LOW)
        m.k[rows] = dot(h1, m.wq[1]).astype(LOW)
        m.v[rows] = (dot(h1, m.wq[2]) + b_qv[1:2]).astype(LOW)

    load_x.wait()
    load_wq.wait()

    def project_own(chunk, carry):
        project(m.x_own[part(chunk)], part(chunk))
        return carry

    lax.fori_loop(0, HALF // TILE, project_own, 0)
    x_swap(1).start()

    def project_got(chunk, carry):
        x_swap(chunk).wait_recv()

        @pl.when(chunk == HALF // TILE - 1)
        def _():
            w_swap.start()
            cot_swap(0).start()

        project(m.h1[other(chunk)], other(chunk))
        return carry

    lax.fori_loop(0, HALF // TILE, project_got, 0)

    def set_bias(block):
        shape = (row_len, SPAN)
        key_at = lax.broadcasted_iota(jnp.int32, shape, 0)
        query_at = lax.broadcasted_iota(jnp.int32, shape, 1) + block * SPAN
        allowed = (m.key_code[...] == m.query_seg[block]) | (key_at == query_at)
        m.bias[...] = jnp.where(allowed, 0.0, FAR)

    def block_rows(block):
        return pl.ds(pl.multiple_of(block * SPAN, SPAN), SPAN)

    def attend_scope(vt, scores, raised):
        vt[...] = m.v[...].T

        def block_at(at):
            return (at + blocks // 2) % blocks

        def score(block, pair, slot):
            cols = slice(128 * pair, 128 * pair + 128)
            scores[slot] = nt_dot(m.k[:, cols], split_heads(m.q[block_rows(block), cols]))

        def weigh(slot):
            held, out = scores.at[slot], raised.at[slot]
            top = None
            for keys in strips(row_len):
                here = held[keys] + twice(m.bias[keys])
                top = here if top is None else jnp.maximum(top, here)
            top = jnp.max(fold(top, jnp.maximum), axis=0, keepdims=True)
            whole = None
            for keys in strips(row_len):
                here = jnp.exp(held[keys] + twice(m.bias[keys]) - top)
                out[keys] = here.astype(LOW)
                whole = here if whole is None else whole + here
            return top, jnp.sum(fold(whole, jnp.add), axis=0, keepdims=True)

        def gather(block, pair, slot, top, whole):
            cols = slice(128 * pair, 128 * pair + 128)
            outs = own_blocks(dot(vt[cols], raised[slot]) / whole)
            m.att32[block_rows(block), cols] = outs.T
            m.lse[block, pair : pair + 1] = top + jnp.log(whole)

        def attend(couple, carry):
            @pl.when(couple == blocks // 8)
            def _():
                w_swap.wait_recv()
                w_share.start()

            @pl.when(couple == blocks // 4)
            def _():
                m.att_send[...] = m.att32[pl.ds(HALF, HALF)].astype(LOW)
                att_swap.start()
                w_share.wait_recv()
                w_pass.start()

            held = None
            for at in range(2 * pairs):
                pair, slot = at % pairs, at % 2
                turn = couple * 2 + at // pairs
                block = block_at(turn)
                if pair == 0:
                    set_bias(block)
                if pair + 1 < pairs:
                    score(block, pair + 1, 1 - slot)
                else:
                    score(block_at(jnp.minimum(turn + 1, blocks - 1)), 0, 1 - slot)
                now = weigh(slot)
                if held is not None:
                    gather(*held)
                held = (block, pair, slot, *now)
            gather(*held)
            return carry

        score(block_at(0), 0, 0)
        lax.fori_loop(0, blocks // 2, attend, 0)

    pl.run_scoped(
        attend_scope,
        pltpu.VMEM((width, row_len), LOW),
        pltpu.VMEM((2, row_len, 2 * SPAN), F32),
        pltpu.VMEM((2, row_len, 2 * SPAN), LOW),
    )

    load_w.wait()
    w_pass.wait_recv()
    att_swap.wait_recv()
    cot_swap(1).start()

    def branch(chunk, carry):
        rows = part(chunk)
        got = dot(m.att32[rows].astype(LOW), m.w_mine[...]) + dot(m.att_got[rows], m.w_got[...])
        middle = m.x_own[rows].astype(F32) + got + as_row(b_out)
        m.middle[rows] = middle
        centred, inverse = normal_parts(middle)
        m.h2[rows] = (centred * inverse * as_row(gain2) + as_row(bias2)).astype(LOW)

        @pl.when(chunk == 0)
        def _():
            h2_swap(0).start()

        return carry

    lax.fori_loop(0, HALF // TILE, branch, 0)
    load_cot.wait()

    if rows_m > 2 * hidden:
        m.grads[pl.ds(2 * hidden, rows_m - 2 * hidden)] = jnp.zeros(
            (rows_m - 2 * hidden, WIDE), LOW
        )

    def mlp_scope(act_ref, pre_ref, up_sum):
        def chunks_scope(up, down, pre_buf, d_buf, up_row, ht):
            load_up, load_down = local(0, up_hbm, up), local(1, down_hbm, down)
            load_up.start()
            load_down.start()
            load_up.wait()
            load_down.wait()
            up_sum[...] = jnp.zeros_like(up_sum)
            up_row[...] = as_row(b_up)
            tiles = hidden // HIDDEN

            def through(begin, tokens):
                rows = pl.ds(begin, tokens)

                def enter(tile):
                    cols = slice(tile * HIDDEN, tile * HIDDEN + HIDDEN)
                    pre_buf[tile % 2, :tokens] = dot(m.h2[rows], up[:, cols])
                    d_buf[tile % 2, :tokens] = nt_dot(m.cot[rows], down[cols])

                def bend(tile):
                    cols = slice(tile * HIDDEN, tile * HIDDEN + HIDDEN)
                    shift_up = up_row[:, cols]
                    total = None
                    for at in range(0, tokens, STRIP):
                        pre = pre_buf[tile % 2, at : at + STRIP] + shift_up
                        cdf = 0.5 * (1.0 + lax.erf(pre * 0.7071067811865476))
                        slope = cdf + pre * (jnp.exp(-0.5 * pre * pre) * 0.3989422804014327)
                        d_pre = (d_buf[tile % 2, at : at + STRIP] * slope).astype(LOW)
                        spot = pl.ds(begin + at, STRIP)
                        act_ref[spot, cols] = (pre * cdf).astype(LOW)
                        pre_ref[spot, cols] = d_pre
                        d_pre = d_pre.astype(F32)
                        total = d_pre if total is None else total + d_pre
                    up_sum[:, cols] += column_sum(fold(total, jnp.add))

                enter(0)
                for tile in range(tiles):
                    if tile + 1 < tiles:
                        enter(tile + 1)
                    bend(tile)

            def grad_part(begin, count):
                span = WIDE // 2
                tokens = pl.ds(begin, count)
                ht[:, :count] = m.h2[tokens].T

                def put(rows, cols, value):
                    if begin:
                        value = value + m.grads[rows, cols].astype(F32)
                    m.grads[rows, cols] = value.astype(LOW)

                def grad_step(at, carry):
                    cols = pl.ds(pl.multiple_of(at * span, 128), span)
                    up_rows = pl.ds(pl.multiple_of(at // 2 * WIDE, WIDE), WIDE)
                    up_cols = pl.ds(pl.multiple_of(at % 2 * span, 128), span)
                    put(up_rows, up_cols, dot(ht[:, :count], pre_ref[tokens, cols]))
                    down_rows = pl.ds(pl.multiple_of(hidden + at * span, 128), span)
                    put(down_rows, slice(None), tn_dot(act_ref[tokens, cols], m.cot[tokens]))
                    return carry

                lax.fori_loop(0, hidden // span, grad_step, 0)

            def products_out(begin, tokens):
                rows = pl.ds(begin, tokens)
                return dot(act_ref[rows], down[...]), nt_dot(pre_ref[rows], up[...])

            through(0, HALF)
            h2_swap(1).start()
            for chunk in range(2):
                rows = pl.ds(chunk * TILE, TILE)
                out, m.dh_own[rows] = products_out(chunk * TILE, TILE)
                m.out_sum[rows] = out + m.middle[rows] + as_row(b_down)
            for chunk in range(2):
                begin = HALF + chunk * TILE
                if chunk == 0:
                    grad_part(0, HALF)
                    h2_swap(0).wait_recv()
                    cot_swap(0).wait_recv()
                else:
                    grad_part(HALF, TILE)
                    h2_swap(1).wait_recv()
                    cot_swap(1).wait_recv()
                    dh2_swap(0).start()
                through(begin, TILE)
                if chunk == 1:
                    grad_part(begin, TILE)
                    ring_m.swap_cores()
                    ring_m.begin()
                out, d_h = products_out(begin, TILE)
                sent = pl.ds(chunk * TILE, TILE)
                m.dh2_send[sent] = d_h.astype(LOW)
                m.out_send[sent] = out.astype(LOW)
            dh2_swap(1).start()

        pl.run_scoped(
            chunks_scope,
            pltpu.VMEM((WIDE, hidden), LOW),
            pltpu.VMEM((hidden, WIDE), LOW),
            pltpu.VMEM((2, HALF, HIDDEN), F32),
            pltpu.VMEM((2, HALF, HIDDEN), F32),
            pltpu.VMEM((1, hidden), F32),
            pltpu.VMEM((WIDE, HALF), LOW),
        )
        m.small_ref[...] = jnp.zeros_like(m.small_ref)
        m.small_ref[0:1] = up_sum[:, :WIDE]
        m.small_ref[1:2] = up_sum[:, WIDE:]

    pl.run_scoped(
        mlp_scope,
        pltpu.VMEM((row_len, hidden), LOW),
        pltpu.VMEM((row_len, hidden), LOW),
        pltpu.VMEM((1, hidden), F32),
    )
    begun = 1
    done = begun + blocks // 2 * pairs
    out_rows = width
    att_swap.wait_send()

    def back_scope(d_qkv, dk_acc, dv_acc, kt, ht, scores, d_probs, probs, d_scores):
        kt[...] = m.k[...].T
        dk_acc[...] = jnp.zeros_like(dk_acc)
        dv_acc[...] = jnp.zeros_like(dv_acc)
        heads_of = jnp.where(
            lax.broadcasted_iota(jnp.int32, (8, 128), 1) // HEAD_DIM
            == lax.broadcasted_iota(jnp.int32, (8, 128), 0),
            1.0,
            0.0,
        ).astype(LOW)

        ht[...] = m.h1[...].T
        probs[...] = jnp.zeros_like(probs)
        d_scores[...] = jnp.zeros_like(d_scores)

        def middle_back(chunk):
            dh2_swap(chunk).wait_recv()

            def some_rows(at, carry):
                rows = pl.ds(pl.multiple_of(chunk * TILE + at * SPAN, SPAN), SPAN)
                d_h2 = m.dh_own[rows] + m.dh2_got[rows].astype(F32)
                cot = m.cot[rows].astype(F32)
                centred, inverse = normal_parts(m.middle[rows])
                unit = centred * inverse
                d_middle = cot + norm_back(d_h2, unit, inverse, as_row(gain2))
                m.middle[rows] = d_middle
                d_branch = d_middle.astype(LOW)
                m.d_branch[rows] = d_branch
                m.att_send[rows] = nt_dot(d_branch, m.w_got[...]).astype(LOW)
                m.d_att[rows] = nt_dot(d_branch, m.w_mine[...]).astype(LOW)
                for at, term in enumerate((d_middle, d_h2 * unit, d_h2, cot)):
                    m.small_ref[10 + at : 11 + at] += column_sum(term)
                return carry

            lax.fori_loop(0, TILE // SPAN, some_rows, 0)

        def out_grads():
            def send_rows(pair, carry):
                cols = pl.ds(pl.multiple_of(pair * 128, 128), 128)
                m.go_send[cols] = tn_dot(m.att_got[:, cols], m.d_branch[...]).astype(LOW)
                return carry

            def own_rows(pair, carry):
                cols = pl.ds(pl.multiple_of(pair * 128, 128), 128)
                rows = pl.ds(pl.multiple_of(rows_m + pair * 128, 128), 128)
                held = m.att32[pl.ds(0, HALF), cols].astype(LOW)
                m.grads[rows] = tn_dot(held, m.d_branch[...]).astype(LOW)
                return carry

            lax.fori_loop(0, pairs, send_rows, 0)
            go_pass.start()
            lax.fori_loop(0, pairs, own_rows, 0)

        def out_grads_on():
            go_pass.wait()
            go = m.go_send[w_rows].astype(F32) + m.go_core[...].astype(F32)
            m.go_core[...] = go.astype(LOW)
            go_swap.start()
            out_swap(0).start()
            out_swap(1).start()

        def enter(block, pair, slot):
            rows, cols = block_rows(block), slice(128 * pair, 128 * pair + 128)
            scores[slot] = nt_dot(m.k[:, cols], split_heads(m.q[rows, cols]))
            d_probs[slot] = nt_dot(m.v[:, cols], split_heads(m.d_att[rows, cols]))

        def weigh(block, pair, slot):
            rows, cols = block_rows(block), slice(128 * pair, 128 * pair + 128)
            weighed = m.d_att[rows, cols].astype(F32) * m.att32[rows, cols]
            high = weighed.astype(LOW)
            rest = (weighed - high.astype(F32)).astype(LOW)
            inner = nt_dot(heads_of, high) + nt_dot(heads_of, rest)
            inner = twice_rows(inner)
            lse = m.lse[block, pair : pair + 1]
            for keys in strips(row_len):
                prob = jnp.exp(scores[slot, keys] + twice(m.bias[keys]) - lse)
                probs[slot, keys] = prob.astype(LOW)
                d_scores[slot, keys] = (prob * (d_probs[slot, keys] - inner)).astype(LOW)

        def leave(block, pair, slot):
            rows, cols = block_rows(block), slice(128 * pair, 128 * pair + 128)
            dk_acc[:, cols] += dot(d_scores[slot], split_heads(m.q[rows, cols]))
            dv_acc[:, cols] += dot(probs[slot], split_heads(m.d_att[rows, cols]))
            d_query = own_blocks(dot(kt[cols], d_scores[slot])).T.astype(LOW)
            d_qkv[0, rows, cols] = d_query * jnp.asarray(SCALE, LOW)

        def two_blocks(couple, carry):
            for at in range(2 * pairs):
                block, pair, slot = couple * 2 + at // pairs, at % pairs, at % 2
                before, after = (pair + pairs - 1) % pairs, (pair + 1) % pairs
                block_in = block if pair + 1 < pairs else jnp.minimum(block + 1, blocks - 1)
                block_out = block if pair > 0 else jnp.maximum(block - 1, 0)
                if pair == 0:
                    set_bias(block)
                if at == 2 * pairs - 1:

                    @pl.when(couple == blocks // 8 - 1)
                    def _():
                        middle_back(1)
                        da_swap.start()
                        out_grads()

                    @pl.when(couple == blocks // 4 - 1)
                    def _():
                        da_swap.wait_recv()
                        out_grads_on()

                enter(block_in, after, 1 - slot)
                leave(block_out, before, 1 - slot)
                weigh(block, pair, slot)
                for group in ((0,), (1, 2))[at % 2]:
                    ring_m.stage(group, begun + couple * pairs + at // 2)
            return carry

        middle_back(0)
        enter(0, 0, 0)
        lax.fori_loop(0, blocks // 2, two_blocks, 0)
        leave(blocks - 1, pairs - 1, (blocks * pairs - 1) % 2)
        d_qkv[1] = dk_acc[...].astype(LOW)
        d_qkv[2] = dv_acc[...].astype(LOW)

        for t in range(3):
            full = dot(ht[...], d_qkv[t]).astype(LOW)
            at = rows_m + out_rows + t * width
            m.grads[pl.ds(at, width), pl.ds(0, width)] = full[:width]
            m.grads[pl.ds(at, width), pl.ds(width, width)] = full[width:]
        go_swap.wait_recv()
        own_rows = pl.ds(pl.multiple_of(rows_m + here.core * quarter, 16), quarter)
        own = m.grads[own_rows].astype(F32)
        m.grads[own_rows] = (own + m.go_got[...].astype(F32)).astype(LOW)
        used = out_rows + 3 * width
        if rows_q > used:
            m.grads[pl.ds(rows_m + used, rows_q - used)] = jnp.zeros((rows_q - used, WIDE), LOW)
        ring_q.swap_cores()
        ring_m.stages(done, done + 1)
        ring_q.begin()

        def input_rows(rows):
            terms = [nt_dot(d_qkv[t, rows], m.wq[t]) for t in range(3)]
            return terms[0] + terms[1] + terms[2]

        dh2_swap(0).wait_send()
        dh2_swap(1).wait_send()

        def input_got(chunk, carry):
            m.dh2_send[part(chunk)] = input_rows(other(chunk)).astype(LOW)
            dh1_swap(chunk).start()
            return carry

        lax.fori_loop(0, HALF // TILE, input_got, 0)
        ring_q.stages(1, 2)
        m.small_ref[2:3, :width] = column_sum(d_qkv[0].astype(F32))
        m.small_ref[2:3, width:] = column_sum(d_qkv[2].astype(F32))

        def input_own(chunk, carry):
            m.dh_own[part(chunk)] = input_rows(part(chunk))
            return carry

        lax.fori_loop(0, HALF // TILE, input_own, 0)

    pl.run_scoped(
        back_scope,
        pltpu.VMEM((3, row_len, width), LOW),
        pltpu.VMEM((row_len, width), F32),
        pltpu.VMEM((row_len, width), F32),
        pltpu.VMEM((width, row_len), LOW),
        pltpu.VMEM((WIDE, row_len), LOW),
        pltpu.VMEM((2, row_len, 2 * SPAN), F32),
        pltpu.VMEM((2, row_len, 2 * SPAN), F32),
        pltpu.VMEM((2, row_len, 2 * SPAN), LOW),
        pltpu.VMEM((2, row_len, 2 * SPAN), LOW),
    )

    def both(step, carry):
        for group in range(GROUPS):
            ring_m.stage(group, done + step)
            ring_q.stage(group, step + 1)
        return carry

    left = max(2 * chips - 1 - (done + 1), 0)
    lax.fori_loop(1, left + 1, both, 0)
    out_swap(0).wait_recv()
    out_swap(1).wait_recv()
    out_ref[...] = (m.out_sum[...] + m.out_got[...].astype(F32)).astype(LOW)
    passed = max(chips + 1, left + 2)
    ring_q.stages(left + 2, passed)

    def first_back(chunk, carry):
        rows = part(chunk)
        dh1_swap(chunk).wait_recv()
        d_h1 = m.dh_own[rows] + m.dh2_got[rows].astype(F32)
        centred, inverse = normal_parts(m.x_own[rows].astype(F32))
        unit = centred * inverse
        dx_ref[rows] = (m.middle[rows] + norm_back(d_h1, unit, inverse, as_row(gain1))).astype(LOW)
        m.small_ref[8:9] += column_sum(d_h1 * unit)
        m.small_ref[9:10] += column_sum(d_h1)
        return carry

    lax.fori_loop(0, HALF // TILE, first_back, 0)
    ring_m.arrive()
    writes = []

    def write_out(which, start, rows):
        if not direct:
            spot = pl.ds(start, rows)
            writes.append(local(which, m.result.at[spot], summed_ref.at[spot]))
            writes[-1].start()

    write_out(0, 0, rows_m)
    small.start(m.small_ref)
    at = passed
    for then in (small.core_done, small.mp_done):
        ring_q.stages(at, at + 1)
        then()
        at += 1
    for hop in range(1, 4):
        ring_q.stages(at, at + 1)
        small.hop(hop)
        at += 1
    ring_q.stages(at, 2 * chips - 1)
    small.finish(small_out, 4)
    ring_q.arrive()
    write_out(1, rows_m, rows_q)
    ring_m.drain()
    ring_q.drain()
    for chunk in range(2):
        for copy in (x_swap, cot_swap, h2_swap, out_swap, dh1_swap):
            copy(chunk).wait_send()
    for copy in (w_swap, w_share, w_pass, da_swap, go_swap):
        copy.wait_send()
    for write in writes:
        write.wait()


def whole_block(x, cot, wq, w_out, w_up, w_down, lengths, mask, gain1, bias1, b_qv, b_out, gain2, bias2, b_up, b_down):
    n_dp = lax.axis_size("dp")
    chips = n_dp // 2
    width = w_out.shape[0]
    hidden = w_up.shape[1]
    row_len = 2 * HALF
    rows_m = whole_blocks(2 * hidden, n_dp)
    rows_q = whole_blocks(4 * width, n_dp)
    rows = rows_m + rows_q
    any_spec = pl.BlockSpec(memory_space=pl.ANY)
    vmem = pl.BlockSpec(memory_space=pltpu.VMEM)
    dma = pltpu.SemaphoreType.DMA
    blocks, pairs = row_len // SPAN, width // 128

    def low(*shape):
        return pltpu.VMEM(shape, LOW)

    def full(*shape):
        return pltpu.VMEM(shape, F32)

    scratch = dict(
        x_own=low(HALF, WIDE),
        h1=low(row_len, WIDE),
        cot=low(row_len, WIDE),
        h2=low(row_len, WIDE),
        wq=low(3, WIDE, width),
        w_mine=low(width, WIDE),
        w_got=low(width, WIDE),
        q=low(row_len, width),
        k=low(row_len, width),
        v=low(row_len, width),
        att32=full(row_len, width),
        att_send=low(HALF, width),
        att_got=low(HALF, width),
        lse=full(blocks, pairs, 2 * SPAN),
        key_code=pltpu.VMEM((row_len, 1), jnp.int32),
        query_seg=pltpu.VMEM((blocks, 1, SPAN), jnp.int32),
        bias=full(row_len, SPAN),
        middle=full(HALF, WIDE),
        out_sum=full(HALF, WIDE),
        out_send=low(HALF, WIDE),
        out_got=low(HALF, WIDE),
        dh_own=full(HALF, WIDE),
        dh2_send=low(HALF, WIDE),
        dh2_got=low(HALF, WIDE),
        d_branch=low(HALF, WIDE),
        d_att=low(row_len, width),
        go_send=low(width, WIDE),
        go_core=low(width // 2, WIDE),
        go_got=low(width // 2, WIDE),
        small_ref=full(16, WIDE),
        grads=low(rows, WIDE),
        from_core=low(rows // 2, WIDE),
        result=low(16 if result_in_hbm(chips) else rows, WIDE),
        landed_m=low(chips - 1, rows_m // n_dp, WIDE),
        landed_q=low(chips - 1, rows_q // n_dp, WIDE),
        local_sems=dma((4,)),
        swap_sems=dma((2, 16)),
        pass_sems=dma((6,)),
        own_sems=dma((2, 2 * GROUPS)),
    )
    return pl.pallas_call(
        functools.partial(block_kernel, chips, (rows_m, rows_q)),
        out_shape=(
            jax.ShapeDtypeStruct((rows, WIDE), LOW),
            jax.ShapeDtypeStruct((HALF, WIDE), LOW),
            jax.ShapeDtypeStruct((HALF, WIDE), LOW),
            jax.ShapeDtypeStruct((16, WIDE), F32),
        ),
        in_specs=[any_spec] * 6 + [pl.BlockSpec(memory_space=pltpu.SMEM)] + [vmem] * 9,
        out_specs=(any_spec, vmem, vmem, vmem),
        scratch_shapes=[scratch[name] for name in SCRATCH]
        + segment_sems(chips) * 2
        + small_scratch(chips),
        compiler_params=pltpu.CompilerParams(
            collective_id=0, has_side_effects=True, vmem_limit_bytes=63 * 2**20
        ),
        cost_estimate=pl.CostEstimate(
            flops=int(40e9), bytes_accessed=int(40e6), transcendentals=0
        ),
        name="whole_block",
    )(x, cot, wq, w_out, w_up, w_down, lengths, mask, gain1, bias1, b_qv, b_out, gain2, bias2, b_up, b_down)


def unpack_kernel(base, pieces, sum_ref, small_ref, a_ref, b_ref, *refs):
    low_buf, full_buf, tokens, in_sems, out_sems, copy_sems = refs[-6:]
    up_ref, down_ref, out_ref, qkv_ref, a_out, b_out, up_sum, qv_ref = refs[:8]
    vectors = refs[8:-6]
    span = low_buf.shape[1]
    half = WIDE // 2
    firm = 2 * (WIDE * 2) // span
    starts = [at * span if at < firm else base + (at - firm) * span for at in range(pieces)]
    fetches = [
        pltpu.make_async_copy(sum_ref.at[pl.ds(start, span)], low_buf.at[at], in_sems.at[at])
        for at, start in enumerate(starts)
    ]
    for fetch in fetches:
        fetch.start()
    ins = [
        pltpu.make_async_copy(ref, tokens.at[at], copy_sems.at[0, at])
        for at, ref in enumerate((a_ref, b_ref))
    ]
    outs = [
        pltpu.make_async_copy(tokens.at[at], ref, copy_sems.at[1, at])
        for at, ref in enumerate((a_out, b_out))
    ]
    for copy in ins:
        copy.start()
    writes = []

    def write(at, lane, src, dst):
        writes.append(pltpu.make_async_copy(src, dst, out_sems.at[at, lane]))
        writes[-1].start()

    for at, fetch in enumerate(fetches):
        fetch.wait()
        held = full_buf.at[at]
        held[...] = low_buf[at].astype(F32)
        row = at * span
        if row < 2 * WIDE:
            rows, cols = pl.ds(row % WIDE, span), pl.ds(row // WIDE * WIDE, WIDE)
            write(at, 0, held, up_ref.at[rows, cols])
        elif row < 4 * WIDE:
            write(at, 0, held, down_ref.at[pl.ds(row - 2 * WIDE, span)])
        elif row < 4 * WIDE + half:
            write(at, 0, held, out_ref.at[pl.ds(row - 4 * WIDE, span)])
        else:
            row = row - 4 * WIDE - half
            for side in range(2):
                rows = pl.ds(side * half + row % half, span)
                write(at, side, held.at[:, pl.ds(side * half, half)], qkv_ref.at[row // half, rows])
    for come, go in zip(ins, outs):
        come.wait()
        go.start()
    up_sum[...] = jnp.concatenate([small_ref[0:1], small_ref[1:2]], axis=1).reshape(2 * WIDE)
    qv_ref[0:1] = small_ref[2:3, :half]
    qv_ref[1:2] = small_ref[2:3, half:]
    for at, vector in enumerate(vectors):
        vector[...] = small_ref[8 + at : 9 + at].reshape(WIDE)
    for copy in outs + writes:
        copy.wait()


def unpack(summed, small, block_out, d_block_in, base, hidden, width):
    pieces = 12
    span = WIDE // 2
    any_spec = pl.BlockSpec(memory_space=pl.ANY)
    vmem = pl.BlockSpec(memory_space=pltpu.VMEM)
    shapes = [(WIDE, hidden), (hidden, WIDE), (width, WIDE), (3, WIDE, width)]
    dma = pltpu.SemaphoreType.DMA
    return pl.pallas_call(
        functools.partial(unpack_kernel, base, pieces),
        out_shape=[jax.ShapeDtypeStruct(s, F32) for s in shapes]
        + [jax.ShapeDtypeStruct((HALF, WIDE), LOW)] * 2
        + [jax.ShapeDtypeStruct((hidden,), F32), jax.ShapeDtypeStruct((2, width), F32)]
        + [jax.ShapeDtypeStruct((WIDE,), F32)] * 6,
        in_specs=[any_spec, vmem, any_spec, any_spec],
        out_specs=[any_spec] * 6 + [vmem] * 8,
        scratch_shapes=[
            pltpu.VMEM((pieces, span, WIDE), LOW),
            pltpu.VMEM((pieces, span, WIDE), F32),
            pltpu.VMEM((2, HALF, WIDE), LOW),
            dma((pieces,)),
            dma((pieces, 2)),
            dma((2, 2)),
        ],
        compiler_params=pltpu.CompilerParams(vmem_limit_bytes=62 * 2**20),
        cost_estimate=pl.CostEstimate(flops=int(1e6), bytes_accessed=int(24e6), transcendentals=0),
        name="unpack",
    )(summed, small, block_out, d_block_in)


def local(
    block_in,
    cotangent,
    lengths,
    token_mask,
    ln1_gain,
    ln1_bias,
    w_qkv,
    b_qv,
    w_out,
    b_out,
    ln2_gain,
    ln2_bias,
    w_up,
    b_up,
    w_down,
    b_down,
):
    summed, block_out, d_block_in, small = whole_block(
        block_in,
        cotangent,
        w_qkv.transpose(1, 0, 2),
        w_out,
        w_up,
        w_down,
        lengths,
        token_mask,
        ln1_gain,
        ln1_bias,
        b_qv,
        b_out,
        ln2_gain,
        ln2_bias,
        b_up,
        b_down,
    )
    base = whole_blocks(2 * w_up.shape[1], lax.axis_size("dp"))
    (
        d_w_up,
        d_w_down,
        d_w_out,
        d_w_qkv,
        block_out,
        d_block_in,
        d_b_up,
        d_b_qv,
        d_ln1_gain,
        d_ln1_bias,
        d_b_out,
        d_ln2_gain,
        d_ln2_bias,
        d_b_down,
    ) = unpack(summed, small, block_out, d_block_in, base, w_up.shape[1], w_out.shape[0])
    return (
        block_out,
        d_block_in,
        d_ln1_gain,
        d_ln1_bias,
        d_w_qkv.transpose(1, 0, 2),
        d_b_qv,
        d_w_out,
        d_b_out,
        d_ln2_gain,
        d_ln2_bias,
        d_w_up,
        d_b_up,
        d_w_down,
        d_b_down,
    )


def solution(mesh):
    in_specs = (
        P(("dp", "mp"), None),
        P(("dp", "mp"), None),
        P("dp", None),
        P("dp", None),
        P(),
        P(),
        P(None, None, "mp"),
        P(None, "mp"),
        P("mp", None),
        P(),
        P(),
        P(),
        P(None, "mp"),
        P("mp"),
        P("mp", None),
        P(),
    )
    out_specs = (
        P(("dp", "mp"), None),
        P(("dp", "mp"), None),
        P(),
        P(),
        P(None, None, "mp"),
        P(None, "mp"),
        P("mp", None),
        P(),
        P(),
        P(),
        P(None, "mp"),
        P("mp"),
        P("mp", None),
        P(),
    )
    return jax.shard_map(local, mesh=mesh, in_specs=in_specs, out_specs=out_specs, check_vma=False)
```

profile of v0, /device:TPU:0, one launch (start us, length us, event | category | flops | bytes accessed | tf_op | source)
XLA Modules:
  0.0 196.4 jit_solution(6696198503603406252)
XLA Ops:
  0.7 186.0 %whole_block.1 = (bf16[4608,768]{1,0:T(8,128)(2,1)}, bf16[512,768]{1,0:T(8,128)(2,1)}, bf16[512,768]{1,0:T(8,128)(2,1)}, f32[16,768]{1,0:T(8,128)}) custom-call(bf16[512,768]{1,0:T(8,128)(2,1)} %refs_0_.1, bf16[512,768]{1,0:T(8,128)(2,1)} %refs_1_.1, bf16[3,768,384]{2,1,0:T(8,128)(2,1)} %bitcast.3, bf16[384,768]{1,0:T(8,128)(2,1)} %refs_3_.1, ...), custom_call_target="tpu_custom_call" | custom-call | flops 40000000000 | bytes 40000000 | tf_op jit(solution)/shard_map/whole_block/pallas_call | solution.py:1134
  186.7 9.5 %unpack.1 = (f32[768,1536]{1,0:T(8,128)}, f32[1536,768]{1,0:T(8,128)}, f32[384,768]{1,0:T(8,128)}, f32[3,768,384]{2,1,0:T(8,128)}, bf16[512,768]{1,0:T(8,128)(2,...) custom-call(bf16[4608,768]{1,0:T(8,128)(2,1)} %get-tuple-element.32., ...), custom_call_target="tpu_custom_call" | custom-call | flops 1000000 | bytes 24000000 | tf_op jit(solution)/shard_map/unpack/pallas_call | solution.py:1223
where the time goes:
time: 197 us; the launch traced here: 196 us
  Pallas kernels  196 us (99%)
    pallas_call x1, Pallas kernels, whole_block(): pl.pallas_call(functools.partial(block_kernel, chips, (rows_m, rows_q)),...  186 us
    pallas_call x1, Pallas kernels, unpack(): pl.pallas_call(functools.partial(unpack_kernel, base, pieces), out_shape=...  9.53 us

commit v1 on v0

--- a/solution.py
+++ b/solution.py
@@ -832,7 +832,7 @@
         pltpu.VMEM((1, hidden), F32),
     )
     begun = 1
-    done = begun + blocks // 2 * pairs
+    done = begun + blocks + 2
     out_rows = width
     att_swap.wait_send()
 
@@ -946,8 +946,13 @@
                 enter(block_in, after, 1 - slot)
                 leave(block_out, before, 1 - slot)
                 weigh(block, pair, slot)
-                for group in ((0,), (1, 2))[at % 2]:
-                    ring_m.stage(group, begun + couple * pairs + at // 2)
+                ring_m.stage(pair, begun + block + 2 * jnp.minimum(couple, 1))
+                if at == 2 * pairs - 1:
+
+                    @pl.when(couple == 0)
+                    def _():
+                        ring_m.stages(begun + 2, begun + 4)
+
             return carry
 
         middle_back(0)

time: 197 us -> 192 us (0.975)
  Pallas kernels: 196 us -> 191 us
    pallas_call x1, Pallas kernels: 186 us -> 182 us  [whole_block(): pl.pallas_call(functools.partial(block_kernel, chips, (rows_m, rows_q)),...]
where the time goes in v1:
time: 192 us
  Pallas kernels  191 us (99%)
    pallas_call x1, Pallas kernels, whole_block(): pl.pallas_call(functools.partial(block_kernel, chips, (rows_m, rows_q)),...  182 us
    pallas_call x1, Pallas kernels, unpack(): pl.pallas_call(functools.partial(unpack_kernel, base, pieces), out_shape=...  9.53 us

profile of v1, /device:TPU:0, one launch (start us, length us, event | category | flops | bytes accessed | tf_op | source)
XLA Modules:
  0.0 192.1 jit_solution(8977916590389061891)
XLA Ops:
  0.7 181.7 %whole_block.1 = (bf16[4608,768]{1,0:T(8,128)(2,1)}, bf16[512,768]{1,0:T(8,128)(2,1)}, bf16[512,768]{1,0:T(8,128)(2,1)}, f32[16,768]{1,0:T(8,128)}) custom-call(bf16[512,768]{1,0:T(8,128)(2,1)} %refs_0_.1, bf16[512,768]{1,0:T(8,128)(2,1)} %refs_1_.1, bf16[3,768,384]{2,1,0:T(8,128)(2,1)} %bitcast.3, bf16[384,768]{1,0:T(8,128)(2,1)} %refs_3_.1, ...), custom_call_target="tpu_custom_call" | custom-call | flops 40000000000 | bytes 40000000 | tf_op jit(solution)/shard_map/whole_block/pallas_call | solution.py:1139
  182.4 9.5 %unpack.1 = (f32[768,1536]{1,0:T(8,128)}, f32[1536,768]{1,0:T(8,128)}, f32[384,768]{1,0:T(8,128)}, f32[3,768,384]{2,1,0:T(8,128)}, bf16[512,768]{1,0:T(8,128)(2,...) custom-call(bf16[4608,768]{1,0:T(8,128)(2,1)} %get-tuple-element.32., ...), custom_call_target="tpu_custom_call" | custom-call | flops 1000000 | bytes 24000000 | tf_op jit(solution)/shard_map/unpack/pallas_call | solution.py:1228

commit v2 on v1

--- a/solution.py
+++ b/solution.py
@@ -831,7 +831,7 @@
         pltpu.VMEM((row_len, hidden), LOW),
         pltpu.VMEM((1, hidden), F32),
     )
-    begun = 1
+    begun = 2
     done = begun + blocks + 2
     out_rows = width
     att_swap.wait_send()
@@ -955,6 +955,7 @@
 
             return carry
 
+        ring_m.stages(1, begun)
         middle_back(0)
         enter(0, 0, 0)
         lax.fori_loop(0, blocks // 2, two_blocks, 0)

time: 192 us -> 192 us (level)
  no operation moved by 1% of the time
where the time goes in v2:
time: 192 us
  Pallas kernels  191 us (99%)
    pallas_call x1, Pallas kernels, whole_block(): pl.pallas_call(functools.partial(block_kernel, chips, (rows_m, rows_q)),...  182 us
    pallas_call x1, Pallas kernels, unpack(): pl.pallas_call(functools.partial(unpack_kernel, base, pieces), out_shape=...  9.53 us

profile of v2, /device:TPU:0, one launch (start us, length us, event | category | flops | bytes accessed | tf_op | source)
XLA Modules:
  0.0 192.0 jit_solution(7558016436890462720)
XLA Ops:
  0.7 181.7 %whole_block.1 = (bf16[4608,768]{1,0:T(8,128)(2,1)}, bf16[512,768]{1,0:T(8,128)(2,1)}, bf16[512,768]{1,0:T(8,128)(2,1)}, f32[16,768]{1,0:T(8,128)}) custom-call(bf16[512,768]{1,0:T(8,128)(2,1)} %refs_0_.1, bf16[512,768]{1,0:T(8,128)(2,1)} %refs_1_.1, bf16[3,768,384]{2,1,0:T(8,128)(2,1)} %bitcast.3, bf16[384,768]{1,0:T(8,128)(2,1)} %refs_3_.1, ...), custom_call_target="tpu_custom_call" | custom-call | flops 40000000000 | bytes 40000000 | tf_op jit(solution)/shard_map/whole_block/pallas_call | solution.py:1140
  182.3 9.5 %unpack.1 = (f32[768,1536]{1,0:T(8,128)}, f32[1536,768]{1,0:T(8,128)}, f32[384,768]{1,0:T(8,128)}, f32[3,768,384]{2,1,0:T(8,128)}, bf16[512,768]{1,0:T(8,128)(2,...) custom-call(bf16[4608,768]{1,0:T(8,128)(2,1)} %get-tuple-element.32., ...), custom_call_target="tpu_custom_call" | custom-call | flops 1000000 | bytes 24000000 | tf_op jit(solution)/shard_map/unpack/pallas_call | solution.py:1229
